TPU v7x, 256 devices: a whole 4x4x8 slice. The times are simulated.
256 devices in a mesh: tensor: 4 (over y), req: 64 (over x, z, core).
Axes of the slice: x: 4, y: 4, z: 8, core: 2. Of those that a mesh axis runs over, the one named last changes fastest.
Arguments:
- hidden_in: bfloat16 [256, 8192], P('req')
- attn_gain: float32 [8192], replicated, may hold values from 0.25 to 1.75
- w_query: bfloat16 [8192, 8192], P('req', 'tensor')
- w_keyval: bfloat16 [2, 8192, 1024], P(None, 'req', 'tensor')
- w_output: bfloat16 [8192, 8192], P('tensor', 'req')
- final_gain: float32 [8192], replicated, may hold values from 0.25 to 1.75
- w_head: bfloat16 [8192, 32000], P('tensor', 'req')
- cache_keys: bfloat16 [256, 2048, 8, 128], P('req', None, 'tensor')
- cache_values: bfloat16 [256, 2048, 8, 128], P('req', None, 'tensor'), may hold values from -6 to 6
- cache_lengths: int32 [256], P('req'), may hold values from 256 to 2047, as said below
- premature: bfloat16 [4, 256, 8192], P(None, 'req')
- premature_layer: int32 [256], P('req'), may hold values from 0 to 3
Outputs:
- contrast: float32 [256, 32000], P('tensor', 'req')
Inputs may be any that keep to these rules, and one draw needn't show every extreme that they name: `cache_lengths`: at least 256; some request has exactly 2047.
All inputs are finite; a program needn't handle non-finite values.
Results may differ from a plain program's by a relative error of at most 0.012.
The roundings to bfloat16 on the way count: a program that leaves them out, or rounds other values in their place, can miss the bound.
Values may be sent and summed in bfloat16 or wider, within the bound.
No kernel may reach another device: no remote copies, remote signals or barrier semaphores. Data moves between devices by JAX's collectives and lax.ppermute only.
A program may use at most 64 MiB of HBM per device.

v0:
```python
import math

import jax
import jax.numpy as jnp
from jax import lax
from jax.sharding import PartitionSpec as P

HEAD_DIM = 128


EPSILON = 1e-05


def normalize(values, gain):
    return values * lax.rsqrt(jnp.mean(values * values, axis=-1, keepdims=True) + EPSILON) * gain


def rotate(heads, positions):
    half_dim = heads.shape[-1] // 2
    frequency = jnp.exp(
        -math.log(10000.0) * 2.0 * jnp.arange(half_dim, dtype=jnp.float32) / heads.shape[-1]
    )
    angles = positions[:, None] * frequency[None, :]
    cos_part = jnp.cos(angles)[:, None, :]
    sin_part = jnp.sin(angles)[:, None, :]
    lower_half = heads[..., :half_dim]
    upper_half = heads[..., half_dim:]
    return jnp.concatenate(
        [
            lower_half * cos_part - upper_half * sin_part,
            upper_half * cos_part + lower_half * sin_part,
        ],
        axis=-1,
    )


def shards(
    hidden_in,
    attn_gain,
    w_query,
    w_keyval,
    w_output,
    final_gain,
    w_head,
    cache_keys,
    cache_values,
    cache_lengths,
    premature,
    premature_layer,
):
    req_dev, width_all = hidden_in.shape
    slot_count = cache_keys.shape[1]
    tensor_count = lax.axis_size("tensor")
    tensor_pos = lax.axis_index("tensor")
    slice_width = width_all // tensor_count
    hidden = hidden_in.astype(jnp.float32)
    normed = normalize(hidden, attn_gain).astype(jnp.bfloat16)
    spread = lax.all_to_all(normed, "req", split_axis=1, concat_axis=0, tiled=True)
    query_cols = w_query.shape[1]
    pair_cols = w_keyval.shape[2]
    query_part = jnp.dot(spread, w_query, preferred_element_type=jnp.float32)
    key_part = jnp.dot(spread, w_keyval[0], preferred_element_type=jnp.float32)
    value_part = jnp.dot(spread, w_keyval[1], preferred_element_type=jnp.float32)
    projected = lax.psum_scatter(
        jnp.concatenate([query_part, key_part, value_part], axis=1),
        "req",
        scatter_dimension=0,
        tiled=True,
    )
    heads_dev = query_cols // HEAD_DIM
    kv_dev = pair_cols // HEAD_DIM
    group_size = heads_dev // kv_dev
    queries = projected[:, :query_cols].reshape(req_dev, heads_dev, HEAD_DIM)
    keys_new = projected[:, query_cols : query_cols + pair_cols].reshape(req_dev, kv_dev, HEAD_DIM)
    values_new = (
        projected[:, query_cols + pair_cols :]
        .reshape(req_dev, kv_dev, HEAD_DIM)
        .astype(jnp.bfloat16)
    )
    positions = cache_lengths.astype(jnp.float32)
    rot_queries = rotate(queries, positions).astype(jnp.bfloat16)
    rot_keys = rotate(keys_new, positions).astype(jnp.bfloat16)
    grouped = rot_queries.reshape(req_dev, kv_dev, group_size, HEAD_DIM)
    scores = jnp.einsum(
        "nkgd,nlkd->nkgl", grouped, cache_keys, preferred_element_type=jnp.float32
    ) / math.sqrt(HEAD_DIM)
    own_score = jnp.einsum(
        "nkgd,nkd->nkg", grouped, rot_keys, preferred_element_type=jnp.float32
    ) / math.sqrt(HEAD_DIM)
    valid_mask = jnp.arange(slot_count)[None, :] < cache_lengths[:, None]
    scores = jnp.where(valid_mask[:, None, None, :], scores, -jnp.inf)
    row_peak = jnp.maximum(jnp.max(scores, axis=-1), own_score)
    expo = jnp.exp(scores - row_peak[..., None])
    own_expo = jnp.exp(own_score - row_peak)
    sum_exp = jnp.sum(expo, axis=-1) + own_expo
    weights = (expo / sum_exp[..., None]).astype(jnp.bfloat16)
    own_weight = (own_expo / sum_exp).astype(jnp.bfloat16)
    mixed = jnp.einsum("nkgl,nlkd->nkgd", weights, cache_values, preferred_element_type=jnp.float32)
    mixed = (
        mixed
        + own_weight.astype(jnp.float32)[..., None] * values_new.astype(jnp.float32)[:, :, None, :]
    )
    attended = mixed.reshape(req_dev, heads_dev * HEAD_DIM).astype(jnp.bfloat16)
    partial_value = jnp.dot(
        lax.all_gather(attended, "req", axis=0, tiled=True),
        w_output,
        preferred_element_type=jnp.float32,
    )
    gathered_rows = lax.all_to_all(partial_value, "req", split_axis=0, concat_axis=1, tiled=True)
    chosen = premature_layer[None, :] == jnp.arange(premature.shape[0], dtype=jnp.int32)[:, None]
    early_full = jnp.sum(
        jnp.where(chosen[:, :, None], premature.astype(jnp.float32), jnp.float32(0.0)), axis=0
    )
    update = lax.psum(gathered_rows, "tensor")
    residual = hidden + update
    final_rows = normalize(residual, final_gain).astype(jnp.bfloat16)
    early_rows = normalize(early_full, final_gain).astype(jnp.bfloat16)
    final_part = lax.dynamic_slice_in_dim(final_rows, tensor_pos * slice_width, slice_width, 1)
    early_part = lax.dynamic_slice_in_dim(early_rows, tensor_pos * slice_width, slice_width, 1)
    stacked = jnp.stack([final_part, early_part], axis=0)
    logits = jnp.einsum(
        "srd,dv->srv",
        lax.all_gather(stacked, "req", axis=1, tiled=True),
        w_head,
        preferred_element_type=jnp.float32,
    )
    logits = lax.psum_scatter(logits, "tensor", scatter_dimension=1, tiled=True)
    local_peak = jnp.max(logits, axis=-1)
    global_peak = lax.pmax(local_peak, "req")
    global_sum = lax.psum(jnp.sum(jnp.exp(logits - global_peak[..., None]), axis=-1), "req")
    log_total = global_peak + jnp.log(global_sum)
    shifted = logits - log_total[..., None]
    return shifted[0] - shifted[1]


def solution(mesh):
    placed = (
        P("req", None),
        P(),
        P("req", "tensor"),
        P(None, "req", "tensor"),
        P("tensor", "req"),
        P(),
        P("tensor", "req"),
        P("req", None, "tensor", None),
        P("req", None, "tensor", None),
        P("req"),
        P(None, "req", None),
        P("req"),
    )
    return jax.shard_map(
        shards, mesh=mesh, in_specs=placed, out_specs=P("tensor", "req"), check_vma=False
    )
```

profile of v0, /device:TPU:1, one launch (start us, length us, event | category | flops | bytes accessed | tf_op | source)
XLA Modules:
  0.0 743.0 jit_solution(16331014094266428658)
XLA Ops:
  6.5 1.2 fusion.22
  7.7 0.9 fusion.26
  8.7 22.6 %all_to_all.38 = bf16[4,64,128]{2,0,1:T(4,128)(2,1)S(1)} all-to-all(bf16[4,64,128]{2,0,1:T(4,128)(2,1)S(1)} %fusion.26), channel_id=1, replica_groups=mesh['tensor'=4,'req'=64] {'req'}, dimensions={1} | all-to-all | bytes 131072 | tf_op jit(solution)/shard_map/all_to_all | solution.py:58
  31.2 1.0 fusion.27
  32.3 1.0 fusion.29
  33.3 1.5 fusion.49
  34.7 1.8 pad_maximum_fusion
  36.5 0.0 all-gather.6.cloned.1.call-start
  36.6 0.6 copy-done.4
  37.2 0.6 dynamic-slice
  38.5 0.1 multiply_cosine_fusion
  38.6 0.1 iota_compare_fusion
  38.7 182.9 %all-reduce.6.cloned.1.call-done = f32[256,2560]{1,0:T(8,128)} async-done(((f32[256,2560]{1,0:T(8,128)}), f32[256,2560]{1,0:T(8,128)}) %all-reduce.6.cloned.1.call-update) | async-done | bytes 2621456
  221.6 0.8 dynamic-slice.3
  222.4 0.8 dynamic-slice_bitcast_fusion
  223.2 0.1 subtract_convert_fusion.1
  223.3 0.1 fusion.37
  223.4 0.1 maximum_bitcast_fusion
  223.5 0.2 fusion.41
  223.7 3.5 fusion.48
  227.2 0.2 fusion.19
  227.5 0.8 fusion.43
  228.3 2.9 fusion.16
  231.2 0.6 reshape.149
  231.9 77.4 %all-gather.6.cloned.1.call-done = bf16[64,4,2048]{2,1,0:T(4,128)(2,1)} async-done(((bf16[1,4,2048]{2,1,0:T(4,128)(2,1)}), bf16[64,4,2048]{2,1,0:T(4,128)(2,1)}) %all-gather.6.cloned.1.call-update) | async-done | bytes 1048592 | tf_op jit(solution)/shard_map/all_gather | solution.py:105
  309.3 1.3 reshape.150
  310.6 2.1 fusion.50
  312.8 6.7 all-to-all-start.1
  319.4 0.0 all-reduce.4.cloned.1.call-start
  319.5 0.2 select_reduce_fusion
  319.7 0.2 multiply_reduce_fusion
  319.9 9.9 %all-to-all-done.1 = f32[64,4,128]{2,1,0:T(4,128)S(1)} async-done(((f32[64,4,128]{2,1,0:T(4,128)}), f32[64,4,128]{2,1,0:T(4,128)S(1)}, u32[]{:S(2)}, u32[]{:S(2)}) %all-to-all-start.1) | async-done | bytes 131104 | tf_op jit(solution)/shard_map/all_to_all | solution.py:109
  329.8 0.7 copy-done.2
  330.5 0.0 all-gather.4.cloned.1.call-start
  330.5 39.8 %all-reduce.4.cloned.1.call-done = f32[4,8192]{1,0:T(4,128)} async-done(((f32[4,8192]{1,0:T(4,128)}), f32[4,8192]{1,0:T(4,128)}) %all-reduce.4.cloned.1.call-update) | async-done | bytes 131088 | tf_op jit(solution)/shard_map/psum | solution.py:114
  370.4 1.1 multiply_reduce_fusion.1
  371.5 0.1 fusion.39
  371.6 0.6 copy.37
  372.3 0.0 reduce-scatter.2.cloned.1.call-start
  372.3 80.9 %all-gather.4.cloned.1.call-done = bf16[2,256,2048]{2,0,1:T(2,128)(2,1)} async-done(((bf16[2,4,2048]{2,0,1:T(2,128)(2,1)}), bf16[2,256,2048]{2,0,1:T(2,128)(2,1)}) %all-gather.4.cloned.1.call-update) | async-done | bytes 2097168 | tf_op jit(solution)/shard_map/all_gather | solution.py:123
  453.2 4.1 fusion.10
  457.4 21.5 %reduce-scatter.2.cloned.1.call-done = f32[2,64,500]{2,1,0:T(8,128)} async-done(((f32[2,256,500]{2,1,0:T(8,128)}), f32[2,64,500]{2,1,0:T(8,128)}) %reduce-scatter.2.cloned.1.call-update) | async-done | bytes 256016 | tf_op jit(solution)/shard_map/reduce_scatter | solution.py:127
  478.9 1.0 reduce_max.19
  479.9 126.6 %pmax.7 = f32[2,64]{1,0:T(2,128)S(1)} all-reduce(f32[2,64]{1,0:T(2,128)S(1)} %reduce_max.19), channel_id=1, replica_groups=mesh['tensor'=4,'req'=64] {'req'}, use_global_device_ids=true, to_apply=%region_10.11 | all-reduce | flops 128 | bytes 1024 | tf_op jit(solution)/shard_map/pmax | solution.py:129
  606.5 1.1 exponential_reduce_fusion
  607.7 127.1 %psum.15 = f32[2,64]{1,0:T(2,128)S(1)} all-reduce(f32[2,64]{1,0:T(2,128)S(1)} %exponential_reduce_fusion), channel_id=1, replica_groups=mesh['tensor'=4,'req'=64] {'req'}, use_global_device_ids=true, to_apply=%region_12.13 | all-reduce | flops 128 | bytes 1024 | tf_op jit(solution)/shard_map/psum | solution.py:130
  734.8 1.0 broadcast_subtract_fusion
  735.8 0.7 fusion.25
  (33 shorter events, 0.3 us)
Async XLA Ops:
  6.5 446.7 %copy-start = (bf16[2048,500]{0,1:T(8,128)(2,1)S(1)}, bf16[2048,500]{0,1:T(8,128)(2,1)}, u32[]{:S(2)}) copy-start(bf16[2048,500]{0,1:T(8,128)(2,1)} %param.18) | copy-start | bytes 6144004
  6.5 215.0 %all-reduce.6.cloned.1.call-start = ((), (), s32[]{:S(2)}) async-start(), calls=%async_computation.7 | async-start | bytes 5242880
  36.5 0.7 copy-start.4
  36.5 0.7 copy-start.6
  36.5 272.7 %all-gather.6.cloned.1.call-start = ((), (), s32[]{:S(2)}) async-start(), calls=%async_computation.6 | async-start | bytes 1064960 | tf_op jit(solution)/shard_map/all_gather | solution.py:105
  228.3 3.6 copy-start.5
  231.2 88.3 %copy-start.3 = (bf16[4,4,8192]{2,1,0:T(4,128)(2,1)S(1)}, bf16[4,4,8192]{2,1,0:T(4,128)(2,1)}, u32[]{:S(2)}) copy-start(bf16[4,4,8192]{2,1,0:T(4,128)(2,1)} %param.22) | copy-start | bytes 786436
  231.2 139.2 %copy-start.1 = (bf16[4,8192]{1,0:T(4,128)(2,1)S(1)}, bf16[4,8192]{1,0:T(4,128)(2,1)}, u32[]{:S(2)}) copy-start(bf16[4,8192]{1,0:T(4,128)(2,1)} %param.12) | copy-start | bytes 196612
  231.8 139.6 %dynamic-slice-start = ((f32[8192]{0:T(1024)}, s32[]{:T(128)}), f32[2048]{0:T(1024)S(1)}, s32[]{:S(2)}) async-start(f32[8192]{0:T(1024)} %param.17, s32[]{:T(128)} %select_n.13), calls=%async_computation.8 | async-start | bytes 16896 | tf_op jit(solution)/shard_map/dynamic_slice | solution.py:118
  312.8 17.0 %all-to-all-start.1 = ((f32[64,4,128]{2,1,0:T(4,128)}), f32[64,4,128]{2,1,0:T(4,128)S(1)}, u32[]{:S(2)}, u32[]{:S(2)}) async-start(f32[64,4,128]{2,1,0:T(4,128)} %bitcast.11), calls=%async_computation.1 | async-start | bytes 262144 | tf_op jit(solution)/shard_map/all_to_all | solution.py:109
  319.4 50.9 %all-reduce.4.cloned.1.call-start = ((), (), s32[]{:S(2)}) async-start(), calls=%async_computation.3 | async-start | bytes 262144 | tf_op jit(solution)/shard_map/psum | solution.py:114
  329.8 0.7 copy-start.2
  330.5 122.7 %all-gather.4.cloned.1.call-start = ((), (), s32[]{:S(2)}) async-start(), calls=%async_computation.4 | async-start | bytes 2129920 | tf_op jit(solution)/shard_map/all_gather | solution.py:123
  372.3 106.6 %reduce-scatter.2.cloned.1.call-start = ((), (), s32[]{:S(2)}) async-start(), calls=%async_computation.5 | async-start | bytes 1310720 | tf_op jit(solution)/shard_map/reduce_scatter | solution.py:127
Sparse Core Ops, SparseCore 0:
  36.7 184.8 all-reduce.5
  232.0 77.2 all-gather.5
  330.6 39.7 all-reduce.3
  373.0 80.1 all-gather.3
  457.5 21.3 reduce-scatter.1
where the time goes:
time: 744 us; the launch traced here: 743 us
  waiting for transfers between devices  413 us (56%)
  blocking collectives  276 us (37%)
  matrix products  16.3 us (2%)
  between operations  14 us (2%)
  other arithmetic  10.9 us (1%)
    unnamed x6, waiting for transfers between devices  183 us
    psum x1, blocking collectives, shards(): lax.psum(jnp.sum(jnp.exp(logits - global_peak[..., None]), axis=-1), 'req')  127 us
    pmax x1, blocking collectives, shards(): global_peak = lax.pmax(local_peak, 'req')  127 us
    all_gather x1, waiting for transfers between devices, shards(): lax.all_gather(stacked, 'req', axis=1, tiled=True)  80.9 us
    all_gather x1, waiting for transfers between devices, shards(): lax.all_gather(attended, 'req', axis=0, tiled=True)  77.4 us
    psum x1, waiting for transfers between devices, shards(): update = lax.psum(gathered_rows, 'tensor')  39.8 us
    all_to_all x1, blocking collectives, shards(): lax.all_to_all(normed, 'req', split_axis=1, concat_axis=0, tiled=True)  22.6 us
    reduce_scatter x1, waiting for transfers between devices, shards(): logits = lax.psum_scatter(logits, 'tensor', scatter_dimension=1, tiled=True)  21.5 us
  transfers between devices with their start and end apart: 6, of which 6 were waited for; matrix products, arithmetic and copies ran while one was open for 0% of the time, Pallas kernels for 0%

commit v1 on v0

v1 whole, which is shorter than its diff:
```python
import math

import jax
import jax.numpy as jnp
from jax import lax
from jax.experimental import pallas as pl
from jax.experimental.pallas import tpu as pltpu
from jax.sharding import Mesh
from jax.sharding import PartitionSpec as P

HEAD_DIM = 128
EPSILON = 1e-05
PLANE = ("x", "z", "c")
CHIPS = ("x", "z")
NX, NZ, NC, NT = 4, 8, 2, 4
BF = jnp.bfloat16
F32 = jnp.float32


def normalize(values, gain):
    return values * lax.rsqrt(jnp.mean(values * values, axis=-1, keepdims=True) + EPSILON) * gain


def rotate(heads, positions):
    half_dim = heads.shape[-1] // 2
    frequency = jnp.exp(
        -math.log(10000.0) * 2.0 * jnp.arange(half_dim, dtype=jnp.float32) / heads.shape[-1]
    )
    angles = positions[:, None] * frequency[None, :]
    cos_part = jnp.cos(angles)[:, None, :]
    sin_part = jnp.sin(angles)[:, None, :]
    lower_half = heads[..., :half_dim]
    upper_half = heads[..., half_dim:]
    return jnp.concatenate(
        [
            lower_half * cos_part - upper_half * sin_part,
            upper_half * cos_part + lower_half * sin_part,
        ],
        axis=-1,
    )


def swap_cores(values):
    return lax.ppermute(values, "c", [(0, 1), (1, 0)])


def exchange(values, axes):
    return lax.all_to_all(values, axes, 0, 0, tiled=True)


def by_core(own, other):
    first = lax.axis_index("c") == 0
    return jnp.where(first, own, other), jnp.where(first, other, own)


def in_rows(ref, chips):
    return jnp.concatenate([ref[chip].astype(F32) for chip in chips], axis=0)


def natural_rows(own, other, first, req_dev):
    core_0, core_1 = jnp.where(first, own, other), jnp.where(first, other, own)
    ordered = []
    for z in range(NZ):
        span = slice(z * req_dev, (z + 1) * req_dev)
        ordered += [core_0[span], core_1[span]]
    return jnp.concatenate(ordered, axis=0)


def early_head_kernel(core_ref, own_ref, other_ref, w_ref, out_ref, acc_ref):
    step = pl.program_id(0)

    @pl.when(step == 0)
    def _():
        acc_ref[...] = jnp.zeros_like(acc_ref)

    chips = range(NX * NZ)
    rows = jnp.concatenate([in_rows(own_ref.at[0], chips), in_rows(other_ref.at[0], chips)], axis=0)
    acc_ref[...] += lax.dot_general(
        rows.astype(BF), w_ref[...], (((1,), (1,)), ((), ())), preferred_element_type=F32
    )

    @pl.when(step == pl.num_programs(0) - 1)
    def _():
        req_dev = own_ref.shape[2]
        half = NZ * req_dev
        for x in range(NX):
            own = acc_ref[x * half : (x + 1) * half]
            other = acc_ref[(NX + x) * half : (NX + x + 1) * half]
            out_ref[x] = natural_rows(own, other, core_ref[0] == 0, req_dev)


def early_head(core, own, other, w_head_t):
    quarters, chips, req_dev, width = own.shape
    vocab_dev = w_head_t.shape[0]
    rows = pl.BlockSpec((1, chips, req_dev, width), lambda q: (q, 0, 0, 0))
    group = NZ * NC * req_dev
    return pl.pallas_call(
        early_head_kernel,
        grid=(quarters,),
        out_shape=jax.ShapeDtypeStruct((NX, group, vocab_dev), F32),
        in_specs=[
            pl.BlockSpec(memory_space=pltpu.SMEM),
            rows,
            rows,
            pl.BlockSpec((vocab_dev, width), lambda q: (0, q)),
        ],
        out_specs=pl.BlockSpec((NX, group, vocab_dev), lambda q: (0, 0, 0)),
        scratch_shapes=[pltpu.VMEM((NX * group, vocab_dev), F32)],
        compiler_params=pltpu.CompilerParams(vmem_limit_bytes=24 * 2**20),
        cost_estimate=pl.CostEstimate(
            flops=2 * NX * group * vocab_dev * width * quarters,
            bytes_accessed=2 * vocab_dev * width * quarters,
            transcendentals=0,
        ),
        name="early",
    )(core, own, other, w_head_t)


def project_kernel(core_ref, own_ref, other_ref, w_ref, out_ref):
    req_dev = own_ref.shape[1]
    pieces = [ref[z].astype(F32) for ref in (own_ref, other_ref) for z in range(NZ)]
    rows = jnp.concatenate(pieces, axis=0).astype(BF)
    total = jnp.dot(rows, w_ref[...], preferred_element_type=F32)
    half = total.shape[0] // 2
    first = core_ref[0] == 0
    own, other = total[:half], total[half:]
    core_0, core_1 = jnp.where(first, own, other), jnp.where(first, other, own)
    ordered = []
    for z in range(NZ):
        span = slice(z * req_dev, (z + 1) * req_dev)
        ordered += [core_0[span], core_1[span]]
    out_ref[0] = jnp.concatenate(ordered, axis=0)


def project(core, own, other, w_output):
    _, req_dev, width = own.shape
    cols = w_output.shape[1]
    group = NZ * NC * req_dev
    rows = pl.BlockSpec((NZ, req_dev, width), lambda x: (x, 0, 0))
    return pl.pallas_call(
        project_kernel,
        grid=(NX,),
        out_shape=jax.ShapeDtypeStruct((NX, group, cols), F32),
        in_specs=[
            pl.BlockSpec(memory_space=pltpu.SMEM),
            rows,
            rows,
            pl.BlockSpec((width, cols), lambda x: (0, 0)),
        ],
        out_specs=pl.BlockSpec((1, group, cols), lambda x: (x, 0, 0)),
        compiler_params=pltpu.CompilerParams(vmem_limit_bytes=24 * 2**20),
        cost_estimate=pl.CostEstimate(
            flops=2 * NX * group * cols * width,
            bytes_accessed=4 * NX * group * width,
            transcendentals=0,
        ),
        name="project",
    )(core, own, other, w_output)


def settle_kernel(block_ref, parts_ref, hidden_ref, gain_ref, out_ref):
    residual = jnp.sum(parts_ref[...], axis=0) + hidden_ref[...].astype(F32)
    scaled = (residual * gain_ref[pl.ds(block_ref[0], 1), :]).astype(BF)
    out_ref[...] = jnp.broadcast_to(scaled[None], out_ref.shape)


def settle(block, parts, hidden_rows, final_gain):
    group, cols = hidden_rows.shape
    vmem = pl.BlockSpec(memory_space=pltpu.VMEM)
    return pl.pallas_call(
        settle_kernel,
        out_shape=jax.ShapeDtypeStruct((NX * NZ, group, cols), BF),
        in_specs=[pl.BlockSpec(memory_space=pltpu.SMEM), vmem, vmem, vmem],
        out_specs=vmem,
        compiler_params=pltpu.CompilerParams(vmem_limit_bytes=16 * 2**20),
        name="settle",
    )(block, parts, hidden_rows, final_gain.reshape(-1, cols))


def opening_kernel(
    layer_ref, hidden_ref, attn_gain_ref, final_gain_ref, premature_ref, out_ref, early_ref
):
    hidden = hidden_ref[...].astype(F32)
    normed = normalize(hidden, attn_gain_ref[...])
    joined = jnp.concatenate([normed, hidden], axis=0).astype(BF)
    cols = out_ref.shape[2]
    for block in range(out_ref.shape[0]):
        out_ref[block] = joined[:, block * cols : (block + 1) * cols]
    rows = []
    for row in range(hidden.shape[0]):
        rows.append(premature_ref[layer_ref[row], pl.ds(row, 1), :].astype(F32))
    early = normalize(jnp.concatenate(rows, axis=0), final_gain_ref[...])
    early_ref[...] = early.astype(BF)


def opening_blocks(hidden_in, attn_gain, final_gain, premature, premature_layer):
    req_dev, width_all = hidden_in.shape
    chips = NX * NZ
    vmem = pl.BlockSpec(memory_space=pltpu.VMEM)
    return pl.pallas_call(
        opening_kernel,
        out_shape=(
            jax.ShapeDtypeStruct((chips, 2 * req_dev, width_all // chips), BF),
            jax.ShapeDtypeStruct((req_dev, width_all), BF),
        ),
        in_specs=[pl.BlockSpec(memory_space=pltpu.SMEM), vmem, vmem, vmem, vmem],
        out_specs=(vmem, vmem),
        compiler_params=pltpu.CompilerParams(vmem_limit_bytes=16 * 2**20),
        name="opening",
    )(premature_layer, hidden_in, attn_gain[None], final_gain[None], premature)


def head_kernel(
    core_ref, own_ref, other_ref, gain_ref, *refs
):
    *early_refs, w_hbm_ref, diff_ref, stats_ref, w_ref, arrived = refs
    chips, group, cols = own_ref.shape
    first = core_ref[0] == 0
    pair = NC * cols
    per_copy = chips // arrived.shape[0]
    copies = []
    for k in range(arrived.shape[0]):
        span = pl.ds(k * per_copy * pair, per_copy * pair)
        copies.append(
            pltpu.make_async_copy(w_hbm_ref.at[:, span], w_ref.at[:, span], arrived.at[k])
        )
        copies[-1].start()
    total = None
    squares = jnp.zeros((group, pair), F32)
    for chip in range(chips):
        if chip % per_copy == 0:
            copies[chip // per_copy].wait()
        own, other = own_ref[chip], other_ref[chip]
        final_pair = jnp.concatenate(
            [jnp.where(first, own, other), jnp.where(first, other, own)], axis=1
        )
        gains = [gain_ref[NC * chip + k : NC * chip + k + 1, :] for k in range(NC)]
        unscaled = final_pair.astype(F32) / jnp.concatenate(gains, axis=1)
        squares = squares + unscaled * unscaled
        term = lax.dot_general(
            final_pair,
            w_ref[:, chip * pair : (chip + 1) * pair],
            (((1,), (1,)), ((), ())),
            preferred_element_type=F32,
        )
        total = term if total is None else total + term
    mean = jnp.sum(squares, axis=1, keepdims=True) / (chips * pair)
    final = total * lax.rsqrt(mean + EPSILON)
    early = early_refs[0][...]
    for early_ref in early_refs[1:]:
        early = early + early_ref[...]
    peaks, sums = [], []
    for logits in (final, early):
        peak = jnp.max(logits, axis=1, keepdims=True)
        peaks.append(peak)
        sums.append(jnp.sum(jnp.exp(logits - peak), axis=1, keepdims=True))
    square = (2 * group, 2 * group)
    lines = [
        jnp.broadcast_to(jnp.concatenate(parts, axis=0), square).T[:1] for parts in (peaks, sums)
    ]
    stats_ref[...] = jnp.broadcast_to(jnp.concatenate(lines, axis=0)[None], stats_ref.shape)
    diff_ref[...] = final - early


def head(core, own, other, gain, early, w_head_t):
    _, group, cols = own.shape
    vocab_dev, width_all = w_head_t.shape
    plane_size = NX * NZ * NC
    vmem = pl.BlockSpec(memory_space=pltpu.VMEM)
    return pl.pallas_call(
        head_kernel,
        out_shape=(
            jax.ShapeDtypeStruct((group, vocab_dev), F32),
            jax.ShapeDtypeStruct((plane_size, 2, 2 * group), F32),
        ),
        in_specs=[pl.BlockSpec(memory_space=pltpu.SMEM)]
        + [vmem] * (3 + len(early))
        + [pl.BlockSpec(memory_space=pl.ANY)],
        out_specs=(vmem, vmem),
        scratch_shapes=[pltpu.VMEM((vocab_dev, width_all), BF), pltpu.SemaphoreType.DMA((8,))],
        compiler_params=pltpu.CompilerParams(vmem_limit_bytes=56 * 2**20),
        cost_estimate=pl.CostEstimate(
            flops=2 * group * vocab_dev * width_all,
            bytes_accessed=2 * vocab_dev * width_all,
            transcendentals=2 * group * vocab_dev,
        ),
        name="head",
    )(core, own, other, gain, *early, w_head_t)


def finish_kernel(stats_ref, diff_ref, out_ref):
    group = diff_ref.shape[0]
    peaks = stats_ref[:, 0, :]
    peak = jnp.max(peaks, axis=0, keepdims=True)
    total = jnp.sum(stats_ref[:, 1, :] * jnp.exp(peaks - peak), axis=0, keepdims=True)
    log_total = peak + jnp.log(total)
    offset = log_total[:, :group] - log_total[:, group:]
    offset = jnp.broadcast_to(offset, (group, group)).T[:, :1]
    out_ref[...] = diff_ref[...] - offset


def finish(stats, diff):
    vmem = pl.BlockSpec(memory_space=pltpu.VMEM)
    return pl.pallas_call(
        finish_kernel,
        out_shape=jax.ShapeDtypeStruct(diff.shape, F32),
        in_specs=[vmem, vmem],
        out_specs=vmem,
        compiler_params=pltpu.CompilerParams(vmem_limit_bytes=8 * 2**20),
        name="finish",
    )(stats, diff)


def attend(rot_queries, rot_keys, values_new, cache_keys, cache_values, cache_lengths):
    req_dev, slot_count, kv_dev, _ = cache_keys.shape
    group_size = rot_queries.shape[1] // kv_dev
    grouped = rot_queries.reshape(req_dev, kv_dev, group_size, HEAD_DIM)
    scores = jnp.einsum(
        "nkgd,nlkd->nkgl", grouped, cache_keys, preferred_element_type=jnp.float32
    ) / math.sqrt(HEAD_DIM)
    own_score = jnp.einsum(
        "nkgd,nkd->nkg", grouped, rot_keys, preferred_element_type=jnp.float32
    ) / math.sqrt(HEAD_DIM)
    valid_mask = jnp.arange(slot_count)[None, :] < cache_lengths[:, None]
    scores = jnp.where(valid_mask[:, None, None, :], scores, -jnp.inf)
    row_peak = jnp.maximum(jnp.max(scores, axis=-1), own_score)
    expo = jnp.exp(scores - row_peak[..., None])
    own_expo = jnp.exp(own_score - row_peak)
    sum_exp = jnp.sum(expo, axis=-1) + own_expo
    weights = (expo / sum_exp[..., None]).astype(BF)
    own_weight = (own_expo / sum_exp).astype(BF)
    mixed = jnp.einsum("nkgl,nlkd->nkgd", weights, cache_values, preferred_element_type=jnp.float32)
    mixed = mixed + own_weight.astype(F32)[..., None] * values_new.astype(F32)[:, :, None, :]
    return mixed.reshape(req_dev, kv_dev * group_size * HEAD_DIM).astype(BF)


def shards(
    hidden_in,
    attn_gain,
    w_query,
    w_keyval,
    w_output,
    final_gain,
    w_head,
    cache_keys,
    cache_values,
    cache_lengths,
    premature,
    premature_layer,
):
    req_dev, width_all = hidden_in.shape
    plane_size = NX * NZ * NC
    t_pos = lax.axis_index("t")
    c_pos = lax.axis_index("c")
    plane_pos = lax.axis_index(PLANE)
    cols = width_all // plane_size

    head_t = lax.all_gather(w_head, "t", axis=0, tiled=True).T

    both, early_rows = opening_blocks(
        hidden_in, attn_gain, final_gain, premature, premature_layer
    )
    q_both = jnp.concatenate(by_core(w_query, swap_cores(w_query)), axis=0)
    kv_both = jnp.concatenate(by_core(w_keyval, swap_cores(w_keyval)), axis=1)
    w_both = jnp.concatenate([q_both, kv_both[0], kv_both[1]], axis=1)
    both, w_both = lax.optimization_barrier((exchange(both, CHIPS), w_both))
    group = NZ * NC * req_dev
    normed = both[:, :req_dev].reshape(NX * NZ * req_dev, NC * cols)
    hidden_rows = both[:, req_dev:].reshape(NX, NZ, req_dev, NC, cols)
    hidden_rows = lax.dynamic_index_in_dim(hidden_rows, t_pos, 0, keepdims=False)
    hidden_own = lax.dynamic_index_in_dim(hidden_rows, c_pos, 2, keepdims=False)
    hidden_sent = lax.dynamic_index_in_dim(hidden_rows, 1 - c_pos, 2, keepdims=False)
    hidden_rows = jnp.stack(by_core(hidden_own, swap_cores(hidden_sent)), axis=1)
    hidden_rows = hidden_rows.reshape(group, cols)

    slice_width = width_all // NT
    early_part = lax.dynamic_slice_in_dim(early_rows, t_pos * slice_width, slice_width, 1)
    early_part = early_part.reshape(req_dev, NX, slice_width // NX).transpose(1, 0, 2)
    early_quarters = jnp.broadcast_to(early_part[:, None], (NX, NZ) + early_part.shape[1:])
    early_quarters = early_quarters.reshape(NX * NZ, req_dev, slice_width // NX)

    sums = jnp.dot(normed, w_both, preferred_element_type=F32)
    blocks = sums.astype(BF).reshape(NX * NZ, req_dev, w_both.shape[1])
    summed = exchange(jnp.concatenate([blocks, early_quarters], axis=2), CHIPS)
    projected = jnp.sum(summed[:, :, : w_both.shape[1]].astype(F32), axis=0)
    early = lax.all_gather(summed[:, :, w_both.shape[1] :], "x", axis=0)

    query_cols = w_query.shape[1]
    pair_cols = w_keyval.shape[2]
    heads_dev = query_cols // HEAD_DIM
    kv_dev = pair_cols // HEAD_DIM
    queries = projected[:, :query_cols].reshape(req_dev, heads_dev, HEAD_DIM)
    keys_new = projected[:, query_cols : query_cols + pair_cols].reshape(req_dev, kv_dev, HEAD_DIM)
    values_new = (
        projected[:, query_cols + pair_cols :].reshape(req_dev, kv_dev, HEAD_DIM).astype(BF)
    )
    positions = cache_lengths.astype(F32)
    rot_queries = rotate(queries, positions).astype(BF)
    rot_keys = rotate(keys_new, positions).astype(BF)
    attended = attend(rot_queries, rot_keys, values_new, cache_keys, cache_values, cache_lengths)

    own_rows = exchange(jnp.broadcast_to(attended[None], (NX * NZ,) + attended.shape), CHIPS)
    own_rows, early = lax.optimization_barrier((own_rows, early))
    other_rows = swap_cores(own_rows)
    parts = project(c_pos[None], own_rows, other_rows, w_output)
    parts, early = lax.optimization_barrier((parts, early))
    parts = exchange(parts, ("t",))

    early_sums = early_head(c_pos[None], early, swap_cores(early), w_head.T)
    parts, early_sums = lax.optimization_barrier((parts, early_sums))
    early_parts = []
    for k in range(NT):
        block = lax.dynamic_index_in_dim(early_sums, (t_pos + k) % NT, 0, keepdims=False)
        if k > 0:
            block = lax.ppermute(block, "t", [(t, (t + k) % NT) for t in range(NT)])
        early_parts.append(block)

    scaled = settle(plane_pos[None], parts, hidden_rows, final_gain)
    own_cols = exchange(scaled, CHIPS)
    own_cols, *early_parts = lax.optimization_barrier((own_cols, *early_parts))
    other_cols = swap_cores(own_cols)
    gain = final_gain.reshape(plane_size, cols)
    diff, stats = head(c_pos[None], own_cols, other_cols, gain, early_parts, head_t)

    stats = exchange(stats, PLANE)
    return finish(stats, diff)


def solution(mesh):
    fine = Mesh(mesh.devices.reshape(NT, NX, NZ, NC), ("t", "x", "z", "c"))
    placed = (
        P(PLANE, None),
        P(),
        P(PLANE, "t"),
        P(None, PLANE, "t"),
        P("t", PLANE),
        P(),
        P("t", PLANE),
        P(PLANE, None, "t", None),
        P(PLANE, None, "t", None),
        P(PLANE),
        P(None, PLANE, None),
        P(PLANE),
    )
    return jax.shard_map(
        shards, mesh=fine, in_specs=placed, out_specs=P("t", PLANE), check_vma=False
    )
```

time: 744 us -> 169 us (0.23)
  waiting for transfers between devices: 413 us -> 42.8 us
  blocking collectives: 276 us -> 29.2 us
  starting transfers between devices: 6.84 us -> 50.6 us
  Pallas kernels: 0 us -> 13.3 us
  matrix products: 16.3 us -> 4.93 us
  other arithmetic: 10.9 us -> 2.48 us
    unnamed x6 -> x1, waiting for transfers between devices: 183 us -> 0.71 us
    all_gather x2 -> x1, waiting for transfers between devices: 158 us -> 0.01 us  [shards(): head_t = lax.all_gather(w_head, 't', axis=0, tiled=True).T]
    psum x1 -> x0, blocking collectives: 127 us -> none  [shards(): lax.psum(jnp.sum(jnp.exp(logits - global_peak[..., None]), axis=-1), 'req')]
    pmax x1 -> x0, blocking collectives: 127 us -> none  [shards(): global_peak = lax.pmax(local_peak, 'req')]
    psum x1 -> x0, waiting for transfers between devices: 39.8 us -> none  [shards(): update = lax.psum(gathered_rows, 'tensor')]
    all_to_all x1 -> x5, starting transfers between devices: 6.67 us -> 33 us  [exchange(): return lax.all_to_all(values, axes, 0, 0, tiled=True)]
    all_to_all x1 -> x5, waiting for transfers between devices: 9.9 us -> 34.3 us  [exchange(): return lax.all_to_all(values, axes, 0, 0, tiled=True)]
    reduce_scatter x1 -> x0, waiting for transfers between devices: 21.5 us -> none  [shards(): logits = lax.psum_scatter(logits, 'tensor', scatter_dimension=1, tiled=True)]
  transfers between devices with their start and end apart: 6 -> 15, of which waited for: 6 -> 9; matrix products, arithmetic and copies ran while one was open for 0% -> 6% of each run, Pallas kernels for 0% -> 4%
where the time goes in v1:
time: 169 us; the launch traced here: 168 us
  starting transfers between devices  50.6 us (30%)
  waiting for transfers between devices  42.8 us (25%)
  blocking collectives  29.2 us (17%)
  between operations  13.8 us (8%)
  Pallas kernels  13.3 us (8%)
  local copies, waits for them, and re-layouts  10.8 us (6%)
  matrix products  4.93 us (3%)
  other arithmetic  2.48 us (1%)
    all_to_all x5, waiting for transfers between devices, exchange(): return lax.all_to_all(values, axes, 0, 0, tiled=True)  34.3 us
    all_to_all x5, starting transfers between devices, exchange(): return lax.all_to_all(values, axes, 0, 0, tiled=True)  33 us
    all_to_all x1, blocking collectives, exchange(): return lax.all_to_all(values, axes, 0, 0, tiled=True)  15.6 us
    ppermute x6, starting transfers between devices, swap_cores(): return lax.ppermute(values, 'c', [(0, 1), (1, 0)])  13.8 us
    all_gather x1, blocking collectives, shards(): early = lax.all_gather(summed[:, :, w_both.shape[1]:], 'x', axis=0)  13.6 us
    unnamed x44, local copies, waits for them, and re-layouts  8.59 us
    pallas_call x1, Pallas kernels, head(): pl.pallas_call(head_kernel, out_shape=(jax.ShapeDtypeStruct((group, vocab...  6.41 us
    ppermute x6, waiting for transfers between devices, swap_cores(): return lax.ppermute(values, 'c', [(0, 1), (1, 0)])  4.31 us
  transfers between devices with their start and end apart: 15, of which 9 were waited for; matrix products, arithmetic and copies ran while one was open for 6% of the time, Pallas kernels for 4%

profile of v1, /device:TPU:1, one launch (start us, length us, event | category | flops | bytes accessed | tf_op | source)
XLA Modules:
  0.0 167.9 jit_solution(13907774322336580726)
XLA Ops:
  6.5 0.7 all-gather.3.cloned.1.call-update
  7.3 3.3 %collective-permute-start.1 = (bf16[2,128,256]{2,1,0:T(8,128)(2,1)}, bf16[2,128,256]{2,1,0:T(8,128)(2,1)S(1)}, u32[]{:S(2)}, u32[]{:S(2)}) collective-permute-start(bf16[2,128,256]{2,1,0:T(8,128)(2,1)} %param.15), channel_id=1, source_target_pairs={{0,1},{1,0},{2,3},{3,2},{4,5},{5,4},{6,7},{7,6},{8,9},{9,8},{10,11... | collective-permute-start | bytes 393224 | tf_op jit(solution)/shard_map/ppermute | solution.py:44
  10.7 0.8 copy-done.4
  11.4 0.9 copy-done.6
  12.4 0.8 copy-done.8
  13.2 0.8 copy-done.9
  14.0 0.7 copy-done.10
  14.7 1.4 opening.1
  16.1 9.3 %all-to-all-start = ((bf16[32,8,256]{2,1,0:T(8,128)(2,1)}), bf16[32,8,256]{2,1,0:T(8,128)(2,1)S(1)}, u32[]{:S(2)}, u32[]{:S(2)}) async-start(bf16[32,8,256]{2,1,0:T(8,128)(2,1)} %get-tuple-element.22), calls=%async_computation | async-start | bytes 262144 | tf_op jit(solution)/shard_map/all_to_all | solution.py:48
  25.7 8.8 %all-to-all-done = bf16[32,8,256]{2,1,0:T(8,128)(2,1)S(1)} async-done(((bf16[32,8,256]{2,1,0:T(8,128)(2,1)}), bf16[32,8,256]{2,1,0:T(8,128)(2,1)S(1)}, u32[]{:S(2)}, u32[]{:S(2)}) %all-to-all-start) | async-done | bytes 131104 | tf_op jit(solution)/shard_map/all_to_all | solution.py:48
  34.6 0.3 convolution_convert_fusion
  35.2 1.3 pad_maximum_fusion.1
  36.5 4.4 %all-to-all-start.1 = ((bf16[32,4,3072]{2,1,0:T(4,128)(2,1)}), bf16[32,4,3072]{2,1,0:T(4,128)(2,1)S(1)}, u32[]{:S(2)}, u32[]{:S(2)}) async-start(bf16[32,4,3072]{2,1,0:T(4,128)(2,1)} %pad_maximum_fusion.1), calls=%async_computation.1 | async-start | bytes 1572864 | tf_op jit(solution)/shard_map/all_to_all | solution.py:48
  41.1 19.4 %all-to-all-done.1 = bf16[32,4,3072]{2,1,0:T(4,128)(2,1)S(1)} async-done(((bf16[32,4,3072]{2,1,0:T(4,128)(2,1)}), bf16[32,4,3072]{2,1,0:T(4,128)(2,1)S(1)}, u32[]{:S(2)}, u32[]{:S(2)}) %all-to-all-start.1) | async-done | bytes 786464 | tf_op jit(solution)/shard_map/all_to_all | solution.py:48
  60.4 0.3 convert_reduce_fusion
  61.2 3.7 %fusion.35 = (f32[4,2,8]{2,1,0:T(2,128)S(1)}, f32[4,2,8,2048]{3,2,1,0:T(8,128)S(1)}) fusion(bf16[4,2048,2,128]{3,2,1,0:T(2,128)(2,1)} %param.19, bf16[4,2,8,64]{3,2,1,0:T(8,128)(2,1)S(1)} %get-tuple-element.54, bf16[4,2,8,64]{3,2,1,0:T(8,128)(2,1)S(1)} %get-tuple-element.53, pred[4,2048]{1,0:T(4,128)(4,1)S(1)} %iota_compare_fusion), kind=kOutput, calls=%fused_computation.67 | convolution fusion | flops 33980352 | bytes 4743424 | tf_op jit(solution)/shard_map/nkgd,nlkd->nkgl/dot_general | solution.py:318
  64.9 0.2 fusion.19
  65.2 0.7 fusion.16
  65.9 1.1 broadcast_in_dim.31
  67.0 7.7 %all-to-all-start.2 = ((bf16[32,4,2048]{2,1,0:T(4,128)(2,1)}), bf16[32,4,2048]{2,1,0:T(4,128)(2,1)S(1)}, u32[]{:S(2)}, u32[]{:S(2)}) async-start(bf16[32,4,2048]{2,1,0:T(4,128)(2,1)} %broadcast_in_dim.31), calls=%async_computation.2 | async-start | bytes 1048576 | tf_op jit(solution)/shard_map/all_to_all | solution.py:48
  74.8 13.6 %all-gather = bf16[128,4,512]{2,1,0:T(4,128)(2,1)S(1)} all-gather(bf16[32,4,512]{2,1,0:T(4,128)(2,1)S(1)} %slice.63), channel_id=2, replica_groups=mesh['t'=4,'x'=4,'z'=8,'c'=2] {'x'}, dimensions={0}, use_global_device_ids=true | all-gather | bytes 655360 | tf_op jit(solution)/shard_map/all_gather | solution.py:386
  88.3 4.6 %collective-permute-start.2 = (bf16[32,4,2048]{2,1,0:T(4,128)(2,1)S(1)}, bf16[32,4,2048]{2,1,0:T(4,128)(2,1)S(1)}, u32[]{:S(2)}, u32[]{:S(2)}) collective-permute-start(bf16[32,4,2048]{2,1,0:T(4,128)(2,1)S(1)} %all-to-all-done.2.own_ref), channel_id=1, source_target_pairs={{0,1},{1,0},{2,3},{3,2},{4,5},{5,4},{6,7},{7,6},{8,9},{9,8},{10,11... | collective-permute-start | bytes 1572872 | tf_op jit(solution)/shard_map/ppermute | solution.py:44
  92.9 1.5 collective-permute-done.2.other_ref
  94.5 1.0 copy-done.1
  95.5 1.9 %project.1 = f32[4,64,128]{2,1,0:T(8,128)} custom-call(s32[1]{0:T(128)} %bitcast.core_ref, bf16[32,4,2048]{2,1,0:T(4,128)(2,1)S(1)} %all-to-all-done.2.own_ref, bf16[32,4,2048]{2,1,0:T(4,128)(2,1)S(1)} %collective-permute-done.2.other_ref, bf16[2048,128]{1,0:T(8,128)(2,1)S(1)} %copy-done.1), custom_call_target="tpu_custom_call" | custom-call | flops 134217728 | bytes 2097152 | tf_op jit(solution)/shard_map/project/pallas_call | solution.py:140
  97.4 0.4 collective-permute-start.3
  98.1 1.2 collective-permute-done.4
  99.4 4.2 %all-to-all-start.3 = ((f32[4,64,128]{2,1,0:T(8,128)}), f32[4,64,128]{2,1,0:T(8,128)S(1)}, u32[]{:S(2)}, u32[]{:S(2)}) async-start(f32[4,64,128]{2,1,0:T(8,128)} %project.1), calls=%async_computation.3 | async-start | bytes 262144 | tf_op jit(solution)/shard_map/all_to_all | solution.py:48
  103.6 0.8 copy-done.2
  104.4 1.0 copy-done.3
  105.4 1.7 %early.1 = f32[4,64,500]{2,1,0:T(8,128)S(1)} custom-call(s32[1]{0:T(128)} %bitcast.core_ref, bf16[4,32,4,512]{3,2,1,0:T(4,128)(2,1)S(1)} %bitcast.61, bf16[4,32,4,512]{3,2,1,0:T(4,128)(2,1)S(1)} %copy-done.3, bf16[500,2048]{1,0:T(8,128)(2,1)S(1)} %bitcast.59), custom_call_target="tpu_custom_call" | custom-call | flops 524288000 | bytes 2048000 | tf_op jit(solution)/shard_map/early/pallas_call | solution.py:97
  107.1 1.2 all-to-all-done.3.parts_ref
  108.4 0.9 settle.1
  109.3 7.4 %all-to-all-start.4 = ((bf16[32,64,128]{2,1,0:T(8,128)(2,1)}), bf16[32,64,128]{2,1,0:T(8,128)(2,1)S(1)}, u32[]{:S(2)}, u32[]{:S(2)}) async-start(bf16[32,64,128]{2,1,0:T(8,128)(2,1)} %settle.1), calls=%async_computation.4 | async-start | bytes 1048576 | tf_op jit(solution)/shard_map/all_to_all | solution.py:48
  116.7 0.7 dynamic-slice_bitcast_fusion
  117.4 0.3 collective-permute-start.5
  117.7 2.3 %collective-permute-start.6 = (f32[64,500]{1,0:T(8,128)S(1)}, f32[64,500]{1,0:T(8,128)S(1)}, u32[]{:S(2)}, u32[]{:S(2)}) collective-permute-start(f32[64,500]{1,0:T(8,128)S(1)} %get-tuple-element.42), channel_id=1, source_target_pairs={{0,128},{64,192},{128,0},{192,64},{1,129},{65,193},{129,1},{193,65... | collective-permute-start | bytes 384008 | tf_op jit(solution)/shard_map/ppermute | solution.py:415
  120.1 1.2 collective-permute-start.7
  121.3 1.2 collective-permute-done.5.refs_1_
  122.5 2.3 %collective-permute-done.6.refs_2_ = f32[64,500]{1,0:T(8,128)S(1)} collective-permute-done((f32[64,500]{1,0:T(8,128)S(1)}, f32[64,500]{1,0:T(8,128)S(1)}, u32[]{:S(2)}, u32[]{:S(2)}) %collective-permute-start.6) | collective-permute-done | bytes 128032 | tf_op jit(solution)/shard_map/ppermute | solution.py:415
  124.8 4.9 %all-to-all-done.4.own_ref = bf16[32,64,128]{2,1,0:T(8,128)(2,1)S(1)} async-done(((bf16[32,64,128]{2,1,0:T(8,128)(2,1)}), bf16[32,64,128]{2,1,0:T(8,128)(2,1)S(1)}, u32[]{:S(2)}, u32[]{:S(2)}) %all-to-all-start.4) | async-done | bytes 524320 | tf_op jit(solution)/shard_map/all_to_all | solution.py:48
  129.7 5.2 %collective-permute-start.8 = (bf16[32,64,128]{2,1,0:T(8,128)(2,1)S(1)}, bf16[32,64,128]{2,1,0:T(8,128)(2,1)S(1)}, u32[]{:S(2)}, u32[]{:S(2)}) collective-permute-start(bf16[32,64,128]{2,1,0:T(8,128)(2,1)S(1)} %all-to-all-done.4.own_ref), channel_id=1, source_target_pairs={{0,1},{1,0},{2,3},{3,2},{4,5},{5,4},{6,7},{7,6},{8,9},{9,8},{10,11... | collective-permute-start | bytes 1572872 | tf_op jit(solution)/shard_map/ppermute | solution.py:44
  134.8 1.5 collective-permute-done.8.other_ref
  136.4 0.8 copy-done.13
  137.2 6.4 %head.1 = (f32[64,500]{1,0:T(8,128)}, f32[64,2,128]{2,1,0:T(2,128)}) custom-call(s32[1]{0:T(128)} %bitcast.core_ref, bf16[32,64,128]{2,1,0:T(8,128)(2,1)} %copy-done.11, bf16[32,64,128]{2,1,0:T(8,128)(2,1)} %copy-done.13, f32[64,128]{1,0:T(8,128)} %bitcast.62, f32[64,500]{1,0:T(8,128)} %get-tuple-element.33.refs_0_, f32[64,500]{1,0:T(8,128)} %copy-done.14, ...), custom_call_target="tpu_custom_call" | custom-call | flops 524288000 | bytes 8192000 | tf_op jit(solution)/shard_map/head/pallas_call | solution.py:270
  143.6 15.6 %all_to_all.30.stats_ref = f32[64,2,128]{2,1,0:T(2,128)S(1)} all-to-all(f32[64,2,128]{2,1,0:T(2,128)} %get-tuple-element.37), channel_id=1, replica_groups=mesh['t'=4,'x'=4,'z'=8,'c'=2] {'x','z','c'}, dimensions={0} | all-to-all | bytes 131072 | tf_op jit(solution)/shard_map/all_to_all | solution.py:48
  159.2 0.9 copy-done.7
  160.1 1.0 finish.1
  (72 shorter events, 1.7 us)
Async XLA Ops:
  6.5 18.9 %copy-start.17 = (bf16[2,128,256]{2,1,0:T(8,128)(2,1)S(1)}, bf16[2,128,256]{2,1,0:T(8,128)(2,1)}, u32[]{:S(2)}) copy-start(bf16[2,128,256]{2,1,0:T(8,128)(2,1)} %param.15) | copy-start | bytes 393220
  6.5 19.0 %copy-start.12 = (bf16[128,2048]{1,0:T(8,128)(2,1)S(1)}, bf16[128,2048]{1,0:T(8,128)(2,1)}, u32[]{:S(2)}) copy-start(bf16[128,2048]{1,0:T(8,128)(2,1)} %param.14) | copy-start | bytes 1572868
  6.5 129.8 %all-gather.3.cloned.1.call-start = ((), (), s32[]{:S(2)}) async-start(), calls=%async_computation.6 | async-start | bytes 10321920 | tf_op jit(solution)/shard_map/all_gather | solution.py:358
  7.3 18.2 %collective-permute-start.1 = (bf16[2,128,256]{2,1,0:T(8,128)(2,1)}, bf16[2,128,256]{2,1,0:T(8,128)(2,1)S(1)}, u32[]{:S(2)}, u32[]{:S(2)}) collective-permute-start(bf16[2,128,256]{2,1,0:T(8,128)(2,1)} %param.15), channel_id=1, source_target_pairs={{0,1},{1,0},{2,3},{3,2},{4,5},{5,4},{6,7},{7,6},{8,9},{9,8},{10,11... | collective-permute-start | bytes 393224 | tf_op jit(solution)/shard_map/ppermute | solution.py:44
  10.6 14.9 %collective-permute-start = (bf16[128,2048]{1,0:T(8,128)(2,1)}, bf16[128,2048]{1,0:T(8,128)(2,1)S(1)}, u32[]{:S(2)}, u32[]{:S(2)}) collective-permute-start(bf16[128,2048]{1,0:T(8,128)(2,1)} %param.14), channel_id=1, source_target_pairs={{0,1},{1,0},{2,3},{3,2},{4,5},{5,4},{6,7},{7,6},{8,9},{9,8},{10,11... | collective-permute-start | bytes 1572872 | tf_op jit(solution)/shard_map/ppermute | solution.py:44
  10.7 0.8 copy-start.4
  11.4 0.9 copy-start.6
  12.4 0.8 copy-start.8
  13.2 0.8 copy-start.9
  14.0 0.7 copy-start.10
  16.1 18.5 %all-to-all-start = ((bf16[32,8,256]{2,1,0:T(8,128)(2,1)}), bf16[32,8,256]{2,1,0:T(8,128)(2,1)S(1)}, u32[]{:S(2)}, u32[]{:S(2)}) async-start(bf16[32,8,256]{2,1,0:T(8,128)(2,1)} %get-tuple-element.22), calls=%async_computation | async-start | bytes 262144 | tf_op jit(solution)/shard_map/all_to_all | solution.py:48
  35.0 5.9 %copy-start.18 = (s32[4]{0:T(128)S(1)}, s32[4]{0:T(128)}, u32[]{:S(2)}) copy-start(s32[4]{0:T(128)} %param.21) | copy-start | bytes 52
  36.5 24.0 %all-to-all-start.1 = ((bf16[32,4,3072]{2,1,0:T(4,128)(2,1)}), bf16[32,4,3072]{2,1,0:T(4,128)(2,1)S(1)}, u32[]{:S(2)}, u32[]{:S(2)}) async-start(bf16[32,4,3072]{2,1,0:T(4,128)(2,1)} %pad_maximum_fusion.1), calls=%async_computation.1 | async-start | bytes 1572864 | tf_op jit(solution)/shard_map/all_to_all | solution.py:48
  61.2 4.0 %copy-start.19 = (bf16[4,2048,2,128]{3,2,1,0:T(2,128)(2,1)S(1)}, bf16[4,2048,2,128]{3,2,1,0:T(2,128)(2,1)}, u32[]{:S(2)}) copy-start(bf16[4,2048,2,128]{3,2,1,0:T(2,128)(2,1)} %param.20) | copy-start | bytes 12582916
  65.9 38.5 %copy-start = (bf16[2048,500]{0,1:T(8,128)(2,1)S(1)}, bf16[2048,500]{0,1:T(8,128)(2,1)}, u32[]{:S(2)}) copy-start(bf16[2048,500]{0,1:T(8,128)(2,1)} %param.18) | copy-start | bytes 6144004
  67.0 21.4 %all-to-all-start.2 = ((bf16[32,4,2048]{2,1,0:T(4,128)(2,1)}), bf16[32,4,2048]{2,1,0:T(4,128)(2,1)S(1)}, u32[]{:S(2)}, u32[]{:S(2)}) async-start(bf16[32,4,2048]{2,1,0:T(4,128)(2,1)} %broadcast_in_dim.31), calls=%async_computation.2 | async-start | bytes 1048576 | tf_op jit(solution)/shard_map/all_to_all | solution.py:48
  88.3 6.1 %collective-permute-start.2 = (bf16[32,4,2048]{2,1,0:T(4,128)(2,1)S(1)}, bf16[32,4,2048]{2,1,0:T(4,128)(2,1)S(1)}, u32[]{:S(2)}, u32[]{:S(2)}) collective-permute-start(bf16[32,4,2048]{2,1,0:T(4,128)(2,1)S(1)} %all-to-all-done.2.own_ref), channel_id=1, source_target_pairs={{0,1},{1,0},{2,3},{3,2},{4,5},{5,4},{6,7},{7,6},{8,9},{9,8},{10,11... | collective-permute-start | bytes 1572872 | tf_op jit(solution)/shard_map/ppermute | solution.py:44
  94.5 1.0 copy-start.1
  95.5 12.8 %copy-start.5 = (f32[8192]{0:T(1024)S(1)}, f32[8192]{0:T(1024)}, u32[]{:S(2)}) copy-start(f32[8192]{0:T(1024)} %param.17) | copy-start | bytes 98308
  97.4 6.1 %collective-permute-start.3 = (bf16[4,32,4,512]{3,2,1,0:T(4,128)(2,1)S(1)}, bf16[4,32,4,512]{3,2,1,0:T(4,128)(2,1)S(1)}, u32[]{:S(2)}, u32[]{:S(2)}) collective-permute-start(bf16[4,32,4,512]{3,2,1,0:T(4,128)(2,1)S(1)} %bitcast.60), channel_id=1, source_target_pairs={{0,1},{1,0},{2,3},{3,2},{4,5},{5,4},{6,7},{7,6},{8,9},{9,8},{10,11... | collective-permute-start | bytes 1572872 | tf_op jit(solution)/shard_map/ppermute | solution.py:44
  97.9 1.4 collective-permute-start.4
  99.4 9.0 %all-to-all-start.3 = ((f32[4,64,128]{2,1,0:T(8,128)}), f32[4,64,128]{2,1,0:T(8,128)S(1)}, u32[]{:S(2)}, u32[]{:S(2)}) async-start(f32[4,64,128]{2,1,0:T(8,128)} %project.1), calls=%async_computation.3 | async-start | bytes 262144 | tf_op jit(solution)/shard_map/all_to_all | solution.py:48
  103.6 0.8 copy-start.2
  104.4 1.0 copy-start.3
  109.3 20.4 %all-to-all-start.4 = ((bf16[32,64,128]{2,1,0:T(8,128)(2,1)}), bf16[32,64,128]{2,1,0:T(8,128)(2,1)S(1)}, u32[]{:S(2)}, u32[]{:S(2)}) async-start(bf16[32,64,128]{2,1,0:T(8,128)(2,1)} %settle.1), calls=%async_computation.4 | async-start | bytes 1048576 | tf_op jit(solution)/shard_map/all_to_all | solution.py:48
  117.4 5.0 %collective-permute-start.5 = (f32[64,500]{1,0:T(8,128)S(1)}, f32[64,500]{1,0:T(8,128)S(1)}, u32[]{:S(2)}, u32[]{:S(2)}) collective-permute-start(f32[64,500]{1,0:T(8,128)S(1)} %get-tuple-element.43), channel_id=1, source_target_pairs={{0,64},{64,128},{128,192},{192,0},{1,65},{65,129},{129,193},{193,1... | collective-permute-start | bytes 384008 | tf_op jit(solution)/shard_map/ppermute | solution.py:415
  117.7 7.0 %collective-permute-start.6 = (f32[64,500]{1,0:T(8,128)S(1)}, f32[64,500]{1,0:T(8,128)S(1)}, u32[]{:S(2)}, u32[]{:S(2)}) collective-permute-start(f32[64,500]{1,0:T(8,128)S(1)} %get-tuple-element.42), channel_id=1, source_target_pairs={{0,128},{64,192},{128,0},{192,64},{1,129},{65,193},{129,1},{193,65... | collective-permute-start | bytes 384008 | tf_op jit(solution)/shard_map/ppermute | solution.py:415
  120.1 4.7 %collective-permute-start.7 = (f32[64,500]{1,0:T(8,128)S(1)}, f32[64,500]{1,0:T(8,128)S(1)}, u32[]{:S(2)}, u32[]{:S(2)}) collective-permute-start(f32[64,500]{1,0:T(8,128)S(1)} %get-tuple-element.41), channel_id=1, source_target_pairs={{0,192},{64,0},{128,64},{192,128},{1,193},{65,1},{129,65},{193,129... | collective-permute-start | bytes 384008 | tf_op jit(solution)/shard_map/ppermute | solution.py:415
  122.5 13.9 %copy-start.14 = (f32[64,500]{1,0:T(8,128)}, f32[64,500]{1,0:T(8,128)S(1)}, u32[]{:S(2)}) copy-start(f32[64,500]{1,0:T(8,128)S(1)} %collective-permute-done.5.refs_1_) | copy-start | bytes 384004
  124.7 11.6 %copy-start.15 = (f32[64,500]{1,0:T(8,128)}, f32[64,500]{1,0:T(8,128)S(1)}, u32[]{:S(2)}) copy-start(f32[64,500]{1,0:T(8,128)S(1)} %collective-permute-done.6.refs_2_) | copy-start | bytes 384004
  124.8 11.6 %copy-start.16 = (f32[64,500]{1,0:T(8,128)}, f32[64,500]{1,0:T(8,128)S(1)}, u32[]{:S(2)}) copy-start(f32[64,500]{1,0:T(8,128)S(1)} %collective-permute-done.7.refs_3_) | copy-start | bytes 384004
  129.7 6.7 %copy-start.11 = (bf16[32,64,128]{2,1,0:T(8,128)(2,1)}, bf16[32,64,128]{2,1,0:T(8,128)(2,1)S(1)}, u32[]{:S(2)}) copy-start(bf16[32,64,128]{2,1,0:T(8,128)(2,1)S(1)} %all-to-all-done.4.own_ref) | copy-start | bytes 1572868
  129.7 6.7 %collective-permute-start.8 = (bf16[32,64,128]{2,1,0:T(8,128)(2,1)S(1)}, bf16[32,64,128]{2,1,0:T(8,128)(2,1)S(1)}, u32[]{:S(2)}, u32[]{:S(2)}) collective-permute-start(bf16[32,64,128]{2,1,0:T(8,128)(2,1)S(1)} %all-to-all-done.4.own_ref), channel_id=1, source_target_pairs={{0,1},{1,0},{2,3},{3,2},{4,5},{5,4},{6,7},{7,6},{8,9},{9,8},{10,11... | collective-permute-start | bytes 1572872 | tf_op jit(solution)/shard_map/ppermute | solution.py:44
  136.4 0.8 copy-start.13
  159.2 0.9 copy-start.7
Sparse Core Ops, SparseCore 0:
  9.2 88.3 all-gather.2

commit v2 on v1

--- a/solution.py
+++ b/solution.py
@@ -178,14 +178,30 @@
 
 
 def opening_kernel(
-    layer_ref, hidden_ref, attn_gain_ref, final_gain_ref, premature_ref, out_ref, early_ref
+    layer_hbm, hidden_hbm, attn_gain_hbm, final_gain_hbm, premature_hbm, out_ref, early_ref,
+    layer_ref, hidden_ref, attn_gain_ref, final_gain_ref, premature_ref, arrived,
 ):
+    pairs = [
+        (hidden_hbm, hidden_ref),
+        (attn_gain_hbm, attn_gain_ref),
+        (premature_hbm, premature_ref),
+        (final_gain_hbm, final_gain_ref),
+        (layer_hbm, layer_ref),
+    ]
+    copies = []
+    for k, (source, target) in enumerate(pairs):
+        copies.append(pltpu.make_async_copy(source, target, arrived.at[k]))
+        copies[-1].start()
+    copies[0].wait()
+    copies[1].wait()
     hidden = hidden_ref[...].astype(F32)
     normed = normalize(hidden, attn_gain_ref[...])
     joined = jnp.concatenate([normed, hidden], axis=0).astype(BF)
     cols = out_ref.shape[2]
     for block in range(out_ref.shape[0]):
         out_ref[block] = joined[:, block * cols : (block + 1) * cols]
+    for copy in copies[2:]:
+        copy.wait()
     rows = []
     for row in range(hidden.shape[0]):
         rows.append(premature_ref[layer_ref[row], pl.ds(row, 1), :].astype(F32))
@@ -203,9 +219,17 @@
             jax.ShapeDtypeStruct((chips, 2 * req_dev, width_all // chips), BF),
             jax.ShapeDtypeStruct((req_dev, width_all), BF),
         ),
-        in_specs=[pl.BlockSpec(memory_space=pltpu.SMEM), vmem, vmem, vmem, vmem],
+        in_specs=[pl.BlockSpec(memory_space=pl.ANY)] * 5,
         out_specs=(vmem, vmem),
-        compiler_params=pltpu.CompilerParams(vmem_limit_bytes=16 * 2**20),
+        scratch_shapes=[
+            pltpu.SMEM(premature_layer.shape, premature_layer.dtype),
+            pltpu.VMEM(hidden_in.shape, hidden_in.dtype),
+            pltpu.VMEM((1, width_all), F32),
+            pltpu.VMEM((1, width_all), F32),
+            pltpu.VMEM(premature.shape, premature.dtype),
+            pltpu.SemaphoreType.DMA((5,)),
+        ],
+        compiler_params=pltpu.CompilerParams(vmem_limit_bytes=60 * 2**20),
         name="opening",
     )(premature_layer, hidden_in, attn_gain[None], final_gain[None], premature)
 
@@ -382,6 +406,7 @@
     sums = jnp.dot(normed, w_both, preferred_element_type=F32)
     blocks = sums.astype(BF).reshape(NX * NZ, req_dev, w_both.shape[1])
     summed = exchange(jnp.concatenate([blocks, early_quarters], axis=2), CHIPS)
+    summed, hidden_rows = lax.optimization_barrier((summed, hidden_rows))
     projected = jnp.sum(summed[:, :, : w_both.shape[1]].astype(F32), axis=0)
     early = lax.all_gather(summed[:, :, w_both.shape[1] :], "x", axis=0)
 

time: 169 us -> 164 us (0.970)
  waiting for transfers between devices: 42.8 us -> 39.3 us
  local copies, waits for them, and re-layouts: 10.8 us -> 7.62 us
  starting transfers between devices: 50.6 us -> 52.9 us
    unnamed x44 -> x34, local copies, waits for them, and re-layouts: 8.59 us -> 4.66 us
    all_to_all x5, waiting for transfers between devices: 34.3 us -> 31.2 us  [exchange(): return lax.all_to_all(values, axes, 0, 0, tiled=True)]
    ppermute x6, starting transfers between devices: 13.8 us -> 16.1 us  [swap_cores(): return lax.ppermute(values, 'c', [(0, 1), (1, 0)])]
  transfers between devices with their start and end apart: 15 -> 15, of which waited for: 9 -> 11; matrix products, arithmetic and copies ran while one was open for 6% -> 6% of each run, Pallas kernels for 4% -> 4%
where the time goes in v2:
time: 164 us; the launch traced here: 163 us
  starting transfers between devices  52.9 us (32%)
  waiting for transfers between devices  39.3 us (24%)
  blocking collectives  28 us (17%)
  Pallas kernels  13.9 us (8%)
  between operations  13.8 us (8%)
  local copies, waits for them, and re-layouts  7.62 us (5%)
  matrix products  4.95 us (3%)
  other arithmetic  2.49 us (2%)
    all_to_all x5, starting transfers between devices, exchange(): return lax.all_to_all(values, axes, 0, 0, tiled=True)  33 us
    all_to_all x5, waiting for transfers between devices, exchange(): return lax.all_to_all(values, axes, 0, 0, tiled=True)  31.2 us
    ppermute x6, starting transfers between devices, swap_cores(): return lax.ppermute(values, 'c', [(0, 1), (1, 0)])  16.1 us
    all_to_all x1, blocking collectives, exchange(): return lax.all_to_all(values, axes, 0, 0, tiled=True)  15.5 us
    all_gather x1, blocking collectives, shards(): early = lax.all_gather(summed[:, :, w_both.shape[1]:], 'x', axis=0)  12.5 us
    pallas_call x1, Pallas kernels, head(): pl.pallas_call(head_kernel, out_shape=(jax.ShapeDtypeStruct((group, vocab...  6.42 us
    unnamed x34, local copies, waits for them, and re-layouts  4.66 us
    ppermute x3, starting transfers between devices, shards(): block = lax.ppermute(block, 't', [(t, (t + k) % NT) for t in range(NT)])  3.81 us
  transfers between devices with their start and end apart: 15, of which 11 were waited for; matrix products, arithmetic and copies ran while one was open for 6% of the time, Pallas kernels for 4%

profile of v2, /device:TPU:1, one launch (start us, length us, event | category | flops | bytes accessed | tf_op | source)
XLA Modules:
  0.0 163.0 jit_solution(12063690546206283126)
XLA Ops:
  6.5 0.7 all-gather.3.cloned.1.call-update
  7.3 3.3 %collective-permute-start.1 = (bf16[2,128,256]{2,1,0:T(8,128)(2,1)}, bf16[2,128,256]{2,1,0:T(8,128)(2,1)S(1)}, u32[]{:S(2)}, u32[]{:S(2)}) collective-permute-start(bf16[2,128,256]{2,1,0:T(8,128)(2,1)} %param.15), channel_id=1, source_target_pairs={{0,1},{1,0},{2,3},{3,2},{4,5},{5,4},{6,7},{7,6},{8,9},{9,8},{10,11... | collective-permute-start | bytes 393224 | tf_op jit(solution)/shard_map/ppermute | solution.py:44
  10.7 2.0 %opening.1 = (bf16[32,8,256]{2,1,0:T(8,128)(2,1)}, bf16[4,8192]{1,0:T(4,128)(2,1)}) custom-call(s32[4]{0:T(128)} %layer_hbm.1, bf16[4,8192]{1,0:T(4,128)(2,1)} %hidden_hbm.1, f32[1,8192]{1,0:T(1,128)} %bitcast.71, f32[1,8192]{1,0:T(1,128)} %bitcast.62, bf16[4,4,8192]{2,1,0:T(4,128)(2,1)} %premature_hbm.1), custom_call_target="tpu_custom_call" | custom-call | tf_op jit(solution)/shard_map/opening/pallas_call | solution.py:216
  12.7 9.3 %all-to-all-start = ((bf16[32,8,256]{2,1,0:T(8,128)(2,1)}), bf16[32,8,256]{2,1,0:T(8,128)(2,1)S(1)}, u32[]{:S(2)}, u32[]{:S(2)}) async-start(bf16[32,8,256]{2,1,0:T(8,128)(2,1)} %get-tuple-element.24), calls=%async_computation | async-start | bytes 262144 | tf_op jit(solution)/shard_map/all_to_all | solution.py:48
  22.0 0.7 constant_dynamic-slice_fusion.2
  23.0 8.1 %all-to-all-done = bf16[32,8,256]{2,1,0:T(8,128)(2,1)S(1)} async-done(((bf16[32,8,256]{2,1,0:T(8,128)(2,1)}), bf16[32,8,256]{2,1,0:T(8,128)(2,1)S(1)}, u32[]{:S(2)}, u32[]{:S(2)}) %all-to-all-start) | async-done | bytes 131104 | tf_op jit(solution)/shard_map/all_to_all | solution.py:48
  31.2 0.3 convolution_convert_fusion
  31.6 0.2 reshape.126
  31.8 1.3 pad_maximum_fusion.1
  33.1 4.4 %all-to-all-start.1 = ((bf16[32,4,3072]{2,1,0:T(4,128)(2,1)}), bf16[32,4,3072]{2,1,0:T(4,128)(2,1)S(1)}, u32[]{:S(2)}, u32[]{:S(2)}) async-start(bf16[32,4,3072]{2,1,0:T(4,128)(2,1)} %pad_maximum_fusion.1), calls=%async_computation.1 | async-start | bytes 1572864 | tf_op jit(solution)/shard_map/all_to_all | solution.py:48
  37.7 1.7 %collective-permute-start.2 = (bf16[8,4,128]{2,0,1:T(8,128)(2,1)S(1)}, bf16[8,4,128]{2,0,1:T(8,128)(2,1)S(1)}, u32[]{:S(2)}, u32[]{:S(2)}) collective-permute-start(bf16[8,4,128]{2,0,1:T(8,128)(2,1)S(1)} %bitcast.74), channel_id=1, source_target_pairs={{0,1},{1,0},{2,3},{3,2},{4,5},{5,4},{6,7},{7,6},{8,9},{9,8},{10,11... | collective-permute-start | bytes 24584 | tf_op jit(solution)/shard_map/ppermute | solution.py:44
  39.5 0.7 collective-permute-done.2
  40.3 16.7 %all-to-all-done.1 = bf16[32,4,3072]{2,1,0:T(4,128)(2,1)S(1)} async-done(((bf16[32,4,3072]{2,1,0:T(4,128)(2,1)}), bf16[32,4,3072]{2,1,0:T(4,128)(2,1)S(1)}, u32[]{:S(2)}, u32[]{:S(2)}) %all-to-all-start.1) | async-done | bytes 786464 | tf_op jit(solution)/shard_map/all_to_all | solution.py:48
  57.0 0.3 convert_reduce_fusion
  57.6 0.2 fusion.27
  57.8 3.7 %fusion.35 = (f32[4,2,8]{2,1,0:T(2,128)S(1)}, f32[4,2,8,2048]{3,2,1,0:T(8,128)S(1)}) fusion(bf16[4,2048,2,128]{3,2,1,0:T(2,128)(2,1)} %param.19, bf16[4,2,8,64]{3,2,1,0:T(8,128)(2,1)S(1)} %get-tuple-element.58, bf16[4,2,8,64]{3,2,1,0:T(8,128)(2,1)S(1)} %get-tuple-element.57, pred[4,2048]{1,0:T(4,128)(4,1)S(1)} %iota_compare_fusion), kind=kOutput, calls=%fused_computation.67 | convolution fusion | flops 33980352 | bytes 4743424 | tf_op jit(solution)/shard_map/nkgd,nlkd->nkgl/dot_general | solution.py:342
  61.5 0.2 fusion.19
  61.7 0.7 fusion.16
  62.5 1.1 broadcast_in_dim.31
  63.6 7.7 %all-to-all-start.2 = ((bf16[32,4,2048]{2,1,0:T(4,128)(2,1)}), bf16[32,4,2048]{2,1,0:T(4,128)(2,1)S(1)}, u32[]{:S(2)}, u32[]{:S(2)}) async-start(bf16[32,4,2048]{2,1,0:T(4,128)(2,1)} %broadcast_in_dim.31), calls=%async_computation.2 | async-start | bytes 1048576 | tf_op jit(solution)/shard_map/all_to_all | solution.py:48
  71.3 12.5 %all-gather = bf16[128,4,512]{2,1,0:T(4,128)(2,1)S(1)} all-gather(bf16[32,4,512]{2,1,0:T(4,128)(2,1)S(1)} %slice.52), channel_id=2, replica_groups=mesh['t'=4,'x'=4,'z'=8,'c'=2] {'x'}, dimensions={0}, use_global_device_ids=true | all-gather | bytes 655360 | tf_op jit(solution)/shard_map/all_gather | solution.py:411
  83.9 0.4 all-to-all-done.2.own_ref
  84.2 5.3 %collective-permute-start.3 = (bf16[32,4,2048]{2,1,0:T(4,128)(2,1)S(1)}, bf16[32,4,2048]{2,1,0:T(4,128)(2,1)S(1)}, u32[]{:S(2)}, u32[]{:S(2)}) collective-permute-start(bf16[32,4,2048]{2,1,0:T(4,128)(2,1)S(1)} %all-to-all-done.2.own_ref), channel_id=1, source_target_pairs={{0,1},{1,0},{2,3},{3,2},{4,5},{5,4},{6,7},{7,6},{8,9},{9,8},{10,11... | collective-permute-start | bytes 1572872 | tf_op jit(solution)/shard_map/ppermute | solution.py:44
  89.5 1.5 collective-permute-done.3.other_ref
  91.0 1.0 copy-done.1
  92.1 1.9 %project.1 = f32[4,64,128]{2,1,0:T(8,128)} custom-call(s32[1]{0:T(128)} %bitcast.core_ref, bf16[32,4,2048]{2,1,0:T(4,128)(2,1)S(1)} %all-to-all-done.2.own_ref, bf16[32,4,2048]{2,1,0:T(4,128)(2,1)S(1)} %collective-permute-done.3.other_ref, bf16[2048,128]{1,0:T(8,128)(2,1)S(1)} %copy-done.1), custom_call_target="tpu_custom_call" | custom-call | flops 134217728 | bytes 2097152 | tf_op jit(solution)/shard_map/project/pallas_call | solution.py:140
  94.0 0.4 collective-permute-start.4
  94.4 4.3 %all-to-all-start.3 = ((f32[4,64,128]{2,1,0:T(8,128)}), f32[4,64,128]{2,1,0:T(8,128)S(1)}, u32[]{:S(2)}, u32[]{:S(2)}) async-start(f32[4,64,128]{2,1,0:T(8,128)} %project.1), calls=%async_computation.3 | async-start | bytes 262144 | tf_op jit(solution)/shard_map/all_to_all | solution.py:48
  98.6 0.8 copy-done.2
  99.5 1.0 copy-done.3
  100.5 1.7 %early.1 = f32[4,64,500]{2,1,0:T(8,128)S(1)} custom-call(s32[1]{0:T(128)} %bitcast.core_ref, bf16[4,32,4,512]{3,2,1,0:T(4,128)(2,1)S(1)} %bitcast.61, bf16[4,32,4,512]{3,2,1,0:T(4,128)(2,1)S(1)} %copy-done.3, bf16[500,2048]{1,0:T(8,128)(2,1)S(1)} %bitcast.59), custom_call_target="tpu_custom_call" | custom-call | flops 524288000 | bytes 2048000 | tf_op jit(solution)/shard_map/early/pallas_call | solution.py:97
  102.2 1.2 all-to-all-done.3.parts_ref
  103.5 0.9 settle.1
  104.4 7.4 %all-to-all-start.4 = ((bf16[32,64,128]{2,1,0:T(8,128)(2,1)}), bf16[32,64,128]{2,1,0:T(8,128)(2,1)S(1)}, u32[]{:S(2)}, u32[]{:S(2)}) async-start(bf16[32,64,128]{2,1,0:T(8,128)(2,1)} %settle.1), calls=%async_computation.4 | async-start | bytes 1048576 | tf_op jit(solution)/shard_map/all_to_all | solution.py:48
  111.8 0.7 dynamic-slice_bitcast_fusion
  112.6 0.4 collective-permute-start.5
  112.9 2.2 %collective-permute-start.6 = (f32[64,500]{1,0:T(8,128)S(1)}, f32[64,500]{1,0:T(8,128)S(1)}, u32[]{:S(2)}, u32[]{:S(2)}) collective-permute-start(f32[64,500]{1,0:T(8,128)S(1)} %get-tuple-element.46), channel_id=1, source_target_pairs={{0,128},{64,192},{128,0},{192,64},{1,129},{65,193},{129,1},{193,65... | collective-permute-start | bytes 384008 | tf_op jit(solution)/shard_map/ppermute | solution.py:440
  115.2 1.2 collective-permute-start.7
  116.4 1.2 collective-permute-done.5.refs_1_
  117.6 2.3 %collective-permute-done.6.refs_2_ = f32[64,500]{1,0:T(8,128)S(1)} collective-permute-done((f32[64,500]{1,0:T(8,128)S(1)}, f32[64,500]{1,0:T(8,128)S(1)}, u32[]{:S(2)}, u32[]{:S(2)}) %collective-permute-start.6) | collective-permute-done | bytes 128032 | tf_op jit(solution)/shard_map/ppermute | solution.py:440
  120.0 4.7 %all-to-all-done.4.own_ref = bf16[32,64,128]{2,1,0:T(8,128)(2,1)S(1)} async-done(((bf16[32,64,128]{2,1,0:T(8,128)(2,1)}), bf16[32,64,128]{2,1,0:T(8,128)(2,1)S(1)}, u32[]{:S(2)}, u32[]{:S(2)}) %all-to-all-start.4) | async-done | bytes 524320 | tf_op jit(solution)/shard_map/all_to_all | solution.py:48
  124.7 5.3 %collective-permute-start.8 = (bf16[32,64,128]{2,1,0:T(8,128)(2,1)S(1)}, bf16[32,64,128]{2,1,0:T(8,128)(2,1)S(1)}, u32[]{:S(2)}, u32[]{:S(2)}) collective-permute-start(bf16[32,64,128]{2,1,0:T(8,128)(2,1)S(1)} %all-to-all-done.4.own_ref), channel_id=1, source_target_pairs={{0,1},{1,0},{2,3},{3,2},{4,5},{5,4},{6,7},{7,6},{8,9},{9,8},{10,11... | collective-permute-start | bytes 1572872 | tf_op jit(solution)/shard_map/ppermute | solution.py:44
  130.0 1.5 collective-permute-done.8.other_ref
  131.6 0.8 copy-done.8
  132.4 6.4 %head.1 = (f32[64,500]{1,0:T(8,128)}, f32[64,2,128]{2,1,0:T(2,128)}) custom-call(s32[1]{0:T(128)} %bitcast.core_ref, bf16[32,64,128]{2,1,0:T(8,128)(2,1)} %copy-done.6, bf16[32,64,128]{2,1,0:T(8,128)(2,1)} %copy-done.8, f32[64,128]{1,0:T(8,128)} %bitcast.63, f32[64,500]{1,0:T(8,128)} %get-tuple-element.37.refs_0_, f32[64,500]{1,0:T(8,128)} %copy-done.9, ...), custom_call_target="tpu_custom_call" | custom-call | flops 524288000 | bytes 8192000 | tf_op jit(solution)/shard_map/head/pallas_call | solution.py:294
  138.8 15.5 %all_to_all.30.stats_ref = f32[64,2,128]{2,1,0:T(2,128)S(1)} all-to-all(f32[64,2,128]{2,1,0:T(2,128)} %get-tuple-element.41), channel_id=1, replica_groups=mesh['t'=4,'x'=4,'z'=8,'c'=2] {'x','z','c'}, dimensions={0} | all-to-all | bytes 131072 | tf_op jit(solution)/shard_map/all_to_all | solution.py:48
  154.3 0.9 copy-done.5
  155.2 1.0 finish.1
  (62 shorter events, 1.2 us)
Async XLA Ops:
  6.5 16.2 %copy-start.12 = (bf16[2,128,256]{2,1,0:T(8,128)(2,1)S(1)}, bf16[2,128,256]{2,1,0:T(8,128)(2,1)}, u32[]{:S(2)}) copy-start(bf16[2,128,256]{2,1,0:T(8,128)(2,1)} %param.15) | copy-start | bytes 393220
  6.5 16.3 %copy-start.7 = (bf16[128,2048]{1,0:T(8,128)(2,1)S(1)}, bf16[128,2048]{1,0:T(8,128)(2,1)}, u32[]{:S(2)}) copy-start(bf16[128,2048]{1,0:T(8,128)(2,1)} %param.14) | copy-start | bytes 1572868
  6.5 125.0 %all-gather.3.cloned.1.call-start = ((), (), s32[]{:S(2)}) async-start(), calls=%async_computation.6 | async-start | bytes 10321920 | tf_op jit(solution)/shard_map/all_gather | solution.py:382
  7.3 15.5 %collective-permute-start.1 = (bf16[2,128,256]{2,1,0:T(8,128)(2,1)}, bf16[2,128,256]{2,1,0:T(8,128)(2,1)S(1)}, u32[]{:S(2)}, u32[]{:S(2)}) collective-permute-start(bf16[2,128,256]{2,1,0:T(8,128)(2,1)} %param.15), channel_id=1, source_target_pairs={{0,1},{1,0},{2,3},{3,2},{4,5},{5,4},{6,7},{7,6},{8,9},{9,8},{10,11... | collective-permute-start | bytes 393224 | tf_op jit(solution)/shard_map/ppermute | solution.py:44
  10.6 12.2 %collective-permute-start = (bf16[128,2048]{1,0:T(8,128)(2,1)}, bf16[128,2048]{1,0:T(8,128)(2,1)S(1)}, u32[]{:S(2)}, u32[]{:S(2)}) collective-permute-start(bf16[128,2048]{1,0:T(8,128)(2,1)} %param.14), channel_id=1, source_target_pairs={{0,1},{1,0},{2,3},{3,2},{4,5},{5,4},{6,7},{7,6},{8,9},{9,8},{10,11... | collective-permute-start | bytes 1572872 | tf_op jit(solution)/shard_map/ppermute | solution.py:44
  12.7 18.5 %all-to-all-start = ((bf16[32,8,256]{2,1,0:T(8,128)(2,1)}), bf16[32,8,256]{2,1,0:T(8,128)(2,1)S(1)}, u32[]{:S(2)}, u32[]{:S(2)}) async-start(bf16[32,8,256]{2,1,0:T(8,128)(2,1)} %get-tuple-element.24), calls=%async_computation | async-start | bytes 262144 | tf_op jit(solution)/shard_map/all_to_all | solution.py:48
  31.6 5.9 %copy-start.13 = (s32[4]{0:T(128)S(1)}, s32[4]{0:T(128)}, u32[]{:S(2)}) copy-start(s32[4]{0:T(128)} %param.21) | copy-start | bytes 52
  33.1 23.9 %all-to-all-start.1 = ((bf16[32,4,3072]{2,1,0:T(4,128)(2,1)}), bf16[32,4,3072]{2,1,0:T(4,128)(2,1)S(1)}, u32[]{:S(2)}, u32[]{:S(2)}) async-start(bf16[32,4,3072]{2,1,0:T(4,128)(2,1)} %pad_maximum_fusion.1), calls=%async_computation.1 | async-start | bytes 1572864 | tf_op jit(solution)/shard_map/all_to_all | solution.py:48
  37.7 2.6 %collective-permute-start.2 = (bf16[8,4,128]{2,0,1:T(8,128)(2,1)S(1)}, bf16[8,4,128]{2,0,1:T(8,128)(2,1)S(1)}, u32[]{:S(2)}, u32[]{:S(2)}) collective-permute-start(bf16[8,4,128]{2,0,1:T(8,128)(2,1)S(1)} %bitcast.74), channel_id=1, source_target_pairs={{0,1},{1,0},{2,3},{3,2},{4,5},{5,4},{6,7},{7,6},{8,9},{9,8},{10,11... | collective-permute-start | bytes 24584 | tf_op jit(solution)/shard_map/ppermute | solution.py:44
  57.8 4.0 %copy-start.14 = (bf16[4,2048,2,128]{3,2,1,0:T(2,128)(2,1)S(1)}, bf16[4,2048,2,128]{3,2,1,0:T(2,128)(2,1)}, u32[]{:S(2)}) copy-start(bf16[4,2048,2,128]{3,2,1,0:T(2,128)(2,1)} %param.20) | copy-start | bytes 12582916
  62.5 37.0 %copy-start = (bf16[2048,500]{0,1:T(8,128)(2,1)S(1)}, bf16[2048,500]{0,1:T(8,128)(2,1)}, u32[]{:S(2)}) copy-start(bf16[2048,500]{0,1:T(8,128)(2,1)} %param.18) | copy-start | bytes 6144004
  63.6 20.6 %all-to-all-start.2 = ((bf16[32,4,2048]{2,1,0:T(4,128)(2,1)}), bf16[32,4,2048]{2,1,0:T(4,128)(2,1)S(1)}, u32[]{:S(2)}, u32[]{:S(2)}) async-start(bf16[32,4,2048]{2,1,0:T(4,128)(2,1)} %broadcast_in_dim.31), calls=%async_computation.2 | async-start | bytes 1048576 | tf_op jit(solution)/shard_map/all_to_all | solution.py:48
  84.2 6.8 %collective-permute-start.3 = (bf16[32,4,2048]{2,1,0:T(4,128)(2,1)S(1)}, bf16[32,4,2048]{2,1,0:T(4,128)(2,1)S(1)}, u32[]{:S(2)}, u32[]{:S(2)}) collective-permute-start(bf16[32,4,2048]{2,1,0:T(4,128)(2,1)S(1)} %all-to-all-done.2.own_ref), channel_id=1, source_target_pairs={{0,1},{1,0},{2,3},{3,2},{4,5},{5,4},{6,7},{7,6},{8,9},{9,8},{10,11... | collective-permute-start | bytes 1572872 | tf_op jit(solution)/shard_map/ppermute | solution.py:44
  91.0 1.0 copy-start.1
  92.1 11.4 %copy-start.4 = (f32[8192]{0:T(1024)S(1)}, f32[8192]{0:T(1024)}, u32[]{:S(2)}) copy-start(f32[8192]{0:T(1024)} %param.17) | copy-start | bytes 98308
  94.0 4.7 %collective-permute-start.4 = (bf16[4,32,4,512]{3,2,1,0:T(4,128)(2,1)S(1)}, bf16[4,32,4,512]{3,2,1,0:T(4,128)(2,1)S(1)}, u32[]{:S(2)}, u32[]{:S(2)}) collective-permute-start(bf16[4,32,4,512]{3,2,1,0:T(4,128)(2,1)S(1)} %bitcast.60), channel_id=1, source_target_pairs={{0,1},{1,0},{2,3},{3,2},{4,5},{5,4},{6,7},{7,6},{8,9},{9,8},{10,11... | collective-permute-start | bytes 1572872 | tf_op jit(solution)/shard_map/ppermute | solution.py:44
  94.4 9.1 %all-to-all-start.3 = ((f32[4,64,128]{2,1,0:T(8,128)}), f32[4,64,128]{2,1,0:T(8,128)S(1)}, u32[]{:S(2)}, u32[]{:S(2)}) async-start(f32[4,64,128]{2,1,0:T(8,128)} %project.1), calls=%async_computation.3 | async-start | bytes 262144 | tf_op jit(solution)/shard_map/all_to_all | solution.py:48
  98.6 0.8 copy-start.2
  99.5 1.0 copy-start.3
  104.4 20.3 %all-to-all-start.4 = ((bf16[32,64,128]{2,1,0:T(8,128)(2,1)}), bf16[32,64,128]{2,1,0:T(8,128)(2,1)S(1)}, u32[]{:S(2)}, u32[]{:S(2)}) async-start(bf16[32,64,128]{2,1,0:T(8,128)(2,1)} %settle.1), calls=%async_computation.4 | async-start | bytes 1048576 | tf_op jit(solution)/shard_map/all_to_all | solution.py:48
  112.6 5.0 %collective-permute-start.5 = (f32[64,500]{1,0:T(8,128)S(1)}, f32[64,500]{1,0:T(8,128)S(1)}, u32[]{:S(2)}, u32[]{:S(2)}) collective-permute-start(f32[64,500]{1,0:T(8,128)S(1)} %get-tuple-element.47), channel_id=1, source_target_pairs={{0,64},{64,128},{128,192},{192,0},{1,65},{65,129},{129,193},{193,1... | collective-permute-start | bytes 384008 | tf_op jit(solution)/shard_map/ppermute | solution.py:440
  112.9 7.0 %collective-permute-start.6 = (f32[64,500]{1,0:T(8,128)S(1)}, f32[64,500]{1,0:T(8,128)S(1)}, u32[]{:S(2)}, u32[]{:S(2)}) collective-permute-start(f32[64,500]{1,0:T(8,128)S(1)} %get-tuple-element.46), channel_id=1, source_target_pairs={{0,128},{64,192},{128,0},{192,64},{1,129},{65,193},{129,1},{193,65... | collective-permute-start | bytes 384008 | tf_op jit(solution)/shard_map/ppermute | solution.py:440
  115.2 4.8 %collective-permute-start.7 = (f32[64,500]{1,0:T(8,128)S(1)}, f32[64,500]{1,0:T(8,128)S(1)}, u32[]{:S(2)}, u32[]{:S(2)}) collective-permute-start(f32[64,500]{1,0:T(8,128)S(1)} %get-tuple-element.45), channel_id=1, source_target_pairs={{0,192},{64,0},{128,64},{192,128},{1,193},{65,1},{129,65},{193,129... | collective-permute-start | bytes 384008 | tf_op jit(solution)/shard_map/ppermute | solution.py:440
  117.6 14.0 %copy-start.9 = (f32[64,500]{1,0:T(8,128)}, f32[64,500]{1,0:T(8,128)S(1)}, u32[]{:S(2)}) copy-start(f32[64,500]{1,0:T(8,128)S(1)} %collective-permute-done.5.refs_1_) | copy-start | bytes 384004
  119.9 11.7 %copy-start.10 = (f32[64,500]{1,0:T(8,128)}, f32[64,500]{1,0:T(8,128)S(1)}, u32[]{:S(2)}) copy-start(f32[64,500]{1,0:T(8,128)S(1)} %collective-permute-done.6.refs_2_) | copy-start | bytes 384004
  120.0 11.6 %copy-start.11 = (f32[64,500]{1,0:T(8,128)}, f32[64,500]{1,0:T(8,128)S(1)}, u32[]{:S(2)}) copy-start(f32[64,500]{1,0:T(8,128)S(1)} %collective-permute-done.7.refs_3_) | copy-start | bytes 384004
  124.7 6.9 %copy-start.6 = (bf16[32,64,128]{2,1,0:T(8,128)(2,1)}, bf16[32,64,128]{2,1,0:T(8,128)(2,1)S(1)}, u32[]{:S(2)}) copy-start(bf16[32,64,128]{2,1,0:T(8,128)(2,1)S(1)} %all-to-all-done.4.own_ref) | copy-start | bytes 1572868
  124.7 6.9 %collective-permute-start.8 = (bf16[32,64,128]{2,1,0:T(8,128)(2,1)S(1)}, bf16[32,64,128]{2,1,0:T(8,128)(2,1)S(1)}, u32[]{:S(2)}, u32[]{:S(2)}) collective-permute-start(bf16[32,64,128]{2,1,0:T(8,128)(2,1)S(1)} %all-to-all-done.4.own_ref), channel_id=1, source_target_pairs={{0,1},{1,0},{2,3},{3,2},{4,5},{5,4},{6,7},{7,6},{8,9},{9,8},{10,11... | collective-permute-start | bytes 1572872 | tf_op jit(solution)/shard_map/ppermute | solution.py:44
  131.6 0.8 copy-start.8
  154.3 0.9 copy-start.5
Sparse Core Ops, SparseCore 0:
  9.2 88.3 all-gather.2
